TPU v7x, 512 devices: a whole 4x4x16 slice. The times are simulated.
512 devices in a mesh: orb: 8 (over y, x_lo), grid: 64 (over x_hi, z, core).
Axes of the slice: x: 4 (x_hi: 2, x_lo: 2; x = x_hi * 2 + x_lo), y: 4, z: 16, core: 2. Of those that a mesh axis runs over, the one named last changes fastest.
Arguments:
- random_orbitals: float32 [8, 256, 256, 256], P('orb', 'grid'), may hold values from -6 to 6
- potential: float32 [256, 256, 256], P('grid'), may hold values from -1.5 to 0.5
- sphere_cells: int32 [1024, 2, 128], P('grid'), may hold values from 0 to 65535, as said below
- projectors: float32 [1024, 4, 128], P('grid'), may hold values from -0.9 to 0.9
- kb_energy: float32 [4], replicated, may hold values from 0.5 to 1.5
- cheb_coef: float32 [3], replicated, may hold values from 0.5 to 1.5
Outputs:
- density: float32 [256, 256, 256], P('grid')
Inputs may be any that keep to these rules, and one draw needn't show every extreme that they name: `sphere_cells`: for each atom a the 128 points are distinct cells: the 128 offsets (dz, dy, dx) with |dz|, |dy|, |dx| <= 3 nearest to the atom's centre, ties broken by the order of (dz, dy, dx) from smallest to largest, added to the centre with periodic wrap along each dimension; row 0 holds the z-plane and row 1 the cell y * 256 + x. The centre's z lies in the slab of planes (a // 16) * 4 to (a // 16) * 4 + 3. Spheres of different atoms may share cells.
All inputs are finite; a program needn't handle non-finite values.
Results may differ from a plain program's by a relative error of at most 0.0002.
Values sent between devices are 32-bit elements; how exact they have to be, the bound alone decides.
A program may use at most 64 MiB of HBM per device.

v0:
```python
import math
import jax
import jax.numpy as jnp
from jax import lax
from jax.sharding import PartitionSpec as P

REACH = 3
PRECISE = lax.Precision.HIGHEST
CENTRE = 2.0
HALF_RANGE = 4.0


def with_halo(cells, sides, width):
    for axis, dim in sides:
        count = lax.axis_size(axis)
        head = lax.slice_in_dim(cells, 0, width, axis=dim)
        tail = lax.slice_in_dim(cells, cells.shape[dim] - width, cells.shape[dim], axis=dim)
        cells = jnp.concatenate(
            [
                lax.ppermute(tail, axis, [(i, (i + 1) % count) for i in range(count)]),
                cells,
                lax.ppermute(head, axis, [((i + 1) % count, i) for i in range(count)]),
            ],
            axis=dim,
        )
    return cells


def from_behind(block, axis, distance):
    devices = range(lax.axis_size(axis))
    route = [((i - distance) % len(devices), i) for i in devices]
    return lax.ppermute(block, axis, route)


def kinetic_table(length):
    places = jnp.arange(length)
    offset = places[:, None] - places[None, :]
    parity = jnp.where(offset % 2 == 0, 1.0, -1.0).astype(jnp.float32)
    angle_half = offset.astype(jnp.float32) * (math.pi / length)
    sine = jnp.where(offset == 0, 1.0, jnp.sin(angle_half))
    off_diag = parity / (2.0 * sine * sine)
    on_diag = jnp.float32(length * length / 12.0 + 1.0 / 6.0)
    return jnp.where(offset == 0, on_diag, off_diag) * (4.0 / (length * length))


def local(random_orbitals, potential, sphere_cells, projectors, kb_energy, cheb_coef):
    grid_count = lax.axis_size("grid")
    grid_pos = lax.axis_index("grid")
    planes = potential.shape[0]
    rows_y = potential.shape[1]
    cols_x = potential.shape[2]
    all_planes = planes * grid_count
    plane_cells = rows_y * cols_x
    first_plane = grid_pos * planes
    orb_count = random_orbitals.shape[0]
    per_dev = sphere_cells.shape[0]
    kinetic_x = kinetic_table(cols_x)
    kinetic_y = kinetic_table(rows_y)
    kinetic_z = kinetic_table(all_planes)

    def along_z(columns):
        turned = jnp.einsum("ozyx,zw->owyx", columns, kinetic_z, precision=PRECISE)
        return lax.all_to_all(turned, "grid", split_axis=1, concat_axis=2, tiled=True)

    z_glob = sphere_cells[:, 0, :]
    in_plane = sphere_cells[:, 1, :]
    local_plane = (z_glob - first_plane + REACH) % all_planes
    ghost_index = (local_plane * plane_cells + in_plane).reshape(-1)

    def nonlocal_term(vector):
        extended = with_halo(vector, (("grid", 1),), REACH)
        flattened = extended.reshape(orb_count, -1)
        values = flattened[:, ghost_index].reshape(orb_count, per_dev, -1)
        coeffs = jnp.einsum("oaj,apj->oap", values, projectors, precision=PRECISE) * kb_energy
        spread = jnp.einsum("oap,apj->oaj", coeffs, projectors, precision=PRECISE).reshape(
            orb_count, -1
        )
        placed = jnp.zeros_like(flattened).at[:, ghost_index].add(spread).reshape(extended.shape)
        lower_rim = placed[:, :REACH]
        upper_rim = placed[:, REACH + planes :]
        from_above = from_behind(lower_rim, "grid", -1)
        from_below = from_behind(upper_rim, "grid", 1)
        interior = placed[:, REACH : REACH + planes]
        interior = interior.at[:, :REACH].add(from_below)
        interior = interior.at[:, planes - REACH :].add(from_above)
        return interior

    def apply_hamiltonian(vector):
        kinetic = jnp.dot(vector.reshape(-1, cols_x), kinetic_x, precision=PRECISE).reshape(
            vector.shape
        )
        kinetic = kinetic + jnp.einsum("ozyx,yw->ozwx", vector, kinetic_y, precision=PRECISE)
        kinetic = kinetic + along_z(
            lax.all_to_all(vector, "grid", split_axis=2, concat_axis=1, tiled=True)
        )
        summed = kinetic + potential * vector + nonlocal_term(vector)
        return (summed - CENTRE * vector) / HALF_RANGE

    first_term = apply_hamiltonian(random_orbitals)
    second_term = 2.0 * apply_hamiltonian(first_term) - random_orbitals
    filtered = (
        cheb_coef[0] * random_orbitals + cheb_coef[1] * first_term + cheb_coef[2] * second_term
    )
    group_density = jnp.sum(filtered * filtered, axis=0)
    density = lax.psum(group_density, "orb")
    return density / (orb_count * lax.axis_size("orb"))


def solution(mesh):
    in_specs = (
        P("orb", "grid", None, None),
        P("grid", None, None),
        P("grid", None, None),
        P("grid", None, None),
        P(),
        P(),
    )
    out_specs = P("grid", None, None)
    return jax.shard_map(local, mesh=mesh, in_specs=in_specs, out_specs=out_specs, check_vma=False)
```

profile of v0, /device:TPU:4, one launch (start us, length us, event | category | flops | bytes accessed | tf_op | source)
XLA Modules:
  0.0 507.4 jit_solution(14557212406994386126)
XLA Ops:
  8.4 70.6 %all_to_all.66 = f32[1,4,256,256]{3,1,0,2:T(4,128)S(1)} all-to-all(f32[1,4,256,256]{3,1,0,2:T(4,128)S(1)} %copy.20), channel_id=1, replica_groups=mesh['orb'=8,'grid'=64] {'grid'}, dimensions={2} | all-to-all | bytes 2097152 | tf_op jit(solution)/shard_map/all_to_all | solution.py:94
  79.6 2.1 convolution_bitcast_fusion.3
  83.3 9.8 %all-to-all-start.1 = ((f32[1,256,4,256]{3,2,0,1:T(4,128)}), f32[1,256,4,256]{3,2,0,1:T(4,128)}, u32[]{:S(2)}, u32[]{:S(2)}) async-start(f32[1,256,4,256]{3,2,0,1:T(4,128)} %copy.22), calls=%async_computation.1 | async-start | bytes 2097152 | tf_op jit(solution)/shard_map/all_to_all | solution.py:63
  94.1 2.0 collective-permute-start
  96.2 7.1 %collective-permute-start.1 = (f32[1,3,256,256]{3,2,1,0:T(8,128)S(1)}, f32[1,3,256,256]{3,2,1,0:T(8,128)S(1)}, u32[]{:S(2)}, u32[]{:S(2)}) collective-permute-start(f32[1,3,256,256]{3,2,1,0:T(8,128)S(1)} %get-tuple-element.60), channel_id=1, source_target_pairs={{1,0},{2,1},{3,2},{4,3},{5,4},{6,5},{7,6},{8,7},{9,8},{10,9},{11,1... | collective-permute-start | bytes 2359304 | tf_op jit(solution)/shard_map/ppermute | solution.py:22
  103.4 46.4 %collective-permute-done = f32[1,3,256,256]{3,2,1,0:T(8,128)S(1)} collective-permute-done((f32[1,3,256,256]{3,2,1,0:T(8,128)}, f32[1,3,256,256]{3,2,1,0:T(8,128)S(1)}, u32[]{:S(2)}, u32[]{:S(2)}) %collective-permute-start) | collective-permute-done | bytes 786464 | tf_op jit(solution)/shard_map/ppermute | solution.py:20
  151.3 11.8 %gather_fusion = f32[2048]{0:T(1024)S(1)} fusion(f32[655360]{0:T(1024)S(1)} %bitcast.161, s32[2048]{0:T(1024)S(1)} %broadcast_clamp_fusion), kind=kCustom, calls=%fused_computation | custom fusion | bytes 24576 | tf_op jit(solution)/shard_map/gather | solution.py:73
  163.7 11.9 %scatter_custom_fusion = f32[655360]{0:T(1024)S(1)} fusion(s32[2048]{0:T(1024)S(1)} %bitcast.173, f32[2048]{0:T(1024)S(1)} %bitcast.182, f32[]{:T(128)} %constant.158.clone.1), kind=kCustom, calls=%fused_computation.14 | custom fusion | flops 2048 | bytes 2621444 | tf_op jit(solution)/shard_map/scatter-add | solution.py:78
  177.5 2.8 fusion.109
  182.2 7.4 %collective-permute-start.3 = (f32[1,3,256,256]{3,2,1,0:T(8,128)}, f32[1,3,256,256]{3,2,1,0:T(8,128)}, u32[]{:S(2)}, u32[]{:S(2)}) collective-permute-start(f32[1,3,256,256]{3,2,1,0:T(8,128)} %get-tuple-element.55), channel_id=1, source_target_pairs={{1,0},{2,1},{3,2},{4,3},{5,4},{6,5},{7,6},{8,7},{9,8},{10,9},{11,1... | collective-permute-start | bytes 2359304 | tf_op jit(solution)/shard_map/ppermute | solution.py:32
  189.7 2.1 convolution_bitcast_fusion.5
  193.1 4.4 collective-permute-done.2
  203.4 5.2 %broadcast_multiply_fusion.1 = (f32[1,4,256,256]{3,2,1,0:T(8,128)S(1)}, f32[1,4,256,256]{3,2,1,0:T(8,128)}) fusion(f32[1,4,256,256]{3,2,1,0:T(8,128)S(1)} %copy-done.2, f32[1,4,256,256]{3,2,1,0:T(8,128)S(1)} %fusion.25, f32[4,256,256]{2,1,0:T(8,128)} %param.15, f32[1,4,256,256]{3,2,1,0:T(8,128)} %all_to_all.54, f32[1,4,256,256]{3,2,1,0:T(8,128)} %bitcast.165), kind=kOutput, calls=%fused_computation.50 | convolution fusion | flops 808910848 | bytes 7340032 | tf_op jit(solution)/shard_map/ozyx,yw->ozwx/dot_general | solution.py:92
  209.2 63.0 %all_to_all.67 = f32[1,4,256,256]{3,1,0,2:T(4,128)S(1)} all-to-all(f32[1,4,256,256]{3,1,0,2:T(4,128)S(1)} %copy.25), channel_id=1, replica_groups=mesh['orb'=8,'grid'=64] {'grid'}, dimensions={2} | all-to-all | bytes 2097152 | tf_op jit(solution)/shard_map/all_to_all | solution.py:94
  272.8 2.1 convolution_bitcast_fusion
  276.6 9.6 %all-to-all-start.3 = ((f32[1,256,4,256]{3,2,0,1:T(4,128)}), f32[1,256,4,256]{3,2,0,1:T(4,128)}, u32[]{:S(2)}, u32[]{:S(2)}) async-start(f32[1,256,4,256]{3,2,0,1:T(4,128)} %copy.27), calls=%async_computation.3 | async-start | bytes 2097152 | tf_op jit(solution)/shard_map/all_to_all | solution.py:63
  286.4 2.1 collective-permute-start.4
  288.4 7.3 %collective-permute-start.5 = (f32[1,3,256,256]{3,2,1,0:T(8,128)S(1)}, f32[1,3,256,256]{3,2,1,0:T(8,128)S(1)}, u32[]{:S(2)}, u32[]{:S(2)}) collective-permute-start(f32[1,3,256,256]{3,2,1,0:T(8,128)S(1)} %get-tuple-element.58), channel_id=1, source_target_pairs={{1,0},{2,1},{3,2},{4,3},{5,4},{6,5},{7,6},{8,7},{9,8},{10,9},{11,1... | collective-permute-start | bytes 2359304 | tf_op jit(solution)/shard_map/ppermute | solution.py:22
  295.8 47.1 %collective-permute-done.4 = f32[1,3,256,256]{3,2,1,0:T(8,128)S(1)} collective-permute-done((f32[1,3,256,256]{3,2,1,0:T(8,128)S(1)}, f32[1,3,256,256]{3,2,1,0:T(8,128)S(1)}, u32[]{:S(2)}, u32[]{:S(2)}) %collective-permute-start.4) | collective-permute-done | bytes 786464 | tf_op jit(solution)/shard_map/ppermute | solution.py:20
  344.5 11.8 %gather_fusion.1 = f32[2048]{0:T(1024)S(1)} fusion(f32[655360]{0:T(1024)S(1)} %bitcast.160, s32[2048]{0:T(1024)S(1)} %broadcast_clamp_fusion), kind=kCustom, calls=%fused_computation.1 | custom fusion | bytes 24576 | tf_op jit(solution)/shard_map/gather | solution.py:73
  356.8 12.9 %scatter_custom_fusion.1 = f32[655360]{0:T(1024)} fusion(s32[2048]{0:T(1024)S(1)} %bitcast.174, f32[2048]{0:T(1024)S(1)} %bitcast.181, f32[]{:T(128)} %constant.158.clone.1), kind=kCustom, calls=%fused_computation.12 | custom fusion | flops 2048 | bytes 2621444 | tf_op jit(solution)/shard_map/scatter-add | solution.py:78
  369.7 2.7 reshape.296
  372.7 2.1 collective-permute-start.6
  374.7 7.3 %collective-permute-start.7 = (f32[1,3,256,256]{3,2,1,0:T(8,128)S(1)}, f32[1,3,256,256]{3,2,1,0:T(8,128)S(1)}, u32[]{:S(2)}, u32[]{:S(2)}) collective-permute-start(f32[1,3,256,256]{3,2,1,0:T(8,128)S(1)} %get-tuple-element.53), channel_id=1, source_target_pairs={{1,0},{2,1},{3,2},{4,3},{5,4},{6,5},{7,6},{8,7},{9,8},{10,9},{11,1... | collective-permute-start | bytes 2359304 | tf_op jit(solution)/shard_map/ppermute | solution.py:32
  383.3 3.1 convolution_bitcast_fusion.1
  387.4 2.3 collective-permute-done.6
  391.5 2.2 fusion.23
  393.7 2.5 copy.46
  396.2 2.6 all_to_all.61
  398.8 6.6 %fusion.21 = f32[4,256,256]{2,1,0:T(8,128)} fusion(f32[1,4,256,256]{3,2,1,0:T(8,128)S(1)} %copy-done.3, f32[1,4,256,256]{3,2,1,0:T(8,128)} %fusion.23, f32[4,256,256]{2,1,0:T(8,128)S(1)} %copy-done.4, f32[1,4,256,256]{3,2,1,0:T(8,128)S(1)} %copy-done.6, f32[]{:T(128)} %bitcast.28, f32[]{:T(128)} %bitcast.27, f32[]{:T(128)} %bitcast, ...), kind=kOutput, calls=%fused_computation.35 | convolution fusion | flops 811270144 | bytes 7340044 | tf_op jit(solution)/shard_map/dot_general | solution.py:89
  405.3 92.9 %all-reduce.2.cloned.1.call-done = f32[4,256,256]{2,1,0:T(8,128)} async-done(((f32[4,256,256]{2,1,0:T(8,128)}), f32[4,256,256]{2,1,0:T(8,128)}) %all-reduce.2.cloned.1.call-update) | async-done | bytes 1048592 | tf_op jit(solution)/shard_map/psum | solution.py:105
  498.2 2.3 broadcast_multiply_fusion
  (63 shorter events, 26.9 us)
Async XLA Ops:
  6.5 156.6 %copy-start = (f32[16,4,128]{2,1,0:T(4,128)S(1)}, f32[16,4,128]{2,1,0:T(4,128)}, u32[]{:S(2)}) copy-start(f32[16,4,128]{2,1,0:T(4,128)} %param.17) | copy-start | bytes 98308
  81.6 11.4 %copy-start.1 = (f32[1,4,256,256]{3,2,1,0:T(8,128)S(1)}, f32[1,4,256,256]{3,2,1,0:T(8,128)}, u32[]{:S(2)}) copy-start(f32[1,4,256,256]{3,2,1,0:T(8,128)} %param.14) | copy-start | bytes 3145732
  83.3 20.0 %copy-start.7 = (s32[16,2,128]{2,1,0:T(2,128)S(1)}, s32[16,2,128]{2,1,0:T(2,128)}, u32[]{:S(2)}) copy-start(s32[16,2,128]{2,1,0:T(2,128)} %param.16) | copy-start | bytes 49156
  83.3 117.3 %all-to-all-start.1 = ((f32[1,256,4,256]{3,2,0,1:T(4,128)}), f32[1,256,4,256]{3,2,0,1:T(4,128)}, u32[]{:S(2)}, u32[]{:S(2)}) async-start(f32[1,256,4,256]{3,2,0,1:T(4,128)} %copy.22), calls=%async_computation.1 | async-start | bytes 2097152 | tf_op jit(solution)/shard_map/all_to_all | solution.py:63
  94.1 55.6 %collective-permute-start = (f32[1,3,256,256]{3,2,1,0:T(8,128)}, f32[1,3,256,256]{3,2,1,0:T(8,128)S(1)}, u32[]{:S(2)}, u32[]{:S(2)}) collective-permute-start(f32[1,3,256,256]{3,2,1,0:T(8,128)} %get-tuple-element.59), channel_id=1, source_target_pairs={{0,1},{1,2},{2,3},{3,4},{4,5},{5,6},{6,7},{7,8},{8,9},{9,10},{10,1... | collective-permute-start | bytes 2359304 | tf_op jit(solution)/shard_map/ppermute | solution.py:20
  96.2 53.6 %collective-permute-start.1 = (f32[1,3,256,256]{3,2,1,0:T(8,128)S(1)}, f32[1,3,256,256]{3,2,1,0:T(8,128)S(1)}, u32[]{:S(2)}, u32[]{:S(2)}) collective-permute-start(f32[1,3,256,256]{3,2,1,0:T(8,128)S(1)} %get-tuple-element.60), channel_id=1, source_target_pairs={{1,0},{2,1},{3,2},{4,3},{5,4},{6,5},{7,6},{8,7},{9,8},{10,9},{11,1... | collective-permute-start | bytes 2359304 | tf_op jit(solution)/shard_map/ppermute | solution.py:22
  151.3 12.1 %copy-start.9 = (f32[4]{0:T(128)S(1)}, f32[4]{0:T(128)}, u32[]{:S(2)}) copy-start(f32[4]{0:T(128)} %param.18) | copy-start | bytes 52
  177.5 12.2 %copy-start.2 = (f32[1,4,256,256]{3,2,1,0:T(8,128)S(1)}, f32[1,4,256,256]{3,2,1,0:T(8,128)}, u32[]{:S(2)}) copy-start(f32[1,4,256,256]{3,2,1,0:T(8,128)} %param.14) | copy-start | bytes 3145732
  180.3 17.2 %collective-permute-start.2 = (f32[1,3,256,256]{3,2,1,0:T(8,128)}, f32[1,3,256,256]{3,2,1,0:T(8,128)}, u32[]{:S(2)}, u32[]{:S(2)}) collective-permute-start(f32[1,3,256,256]{3,2,1,0:T(8,128)} %get-tuple-element.56), channel_id=1, source_target_pairs={{63,0},{0,1},{1,2},{2,3},{3,4},{4,5},{5,6},{6,7},{7,8},{8,9},{9,10... | collective-permute-start | bytes 2359304 | tf_op jit(solution)/shard_map/ppermute | solution.py:32
  182.2 17.1 %collective-permute-start.3 = (f32[1,3,256,256]{3,2,1,0:T(8,128)}, f32[1,3,256,256]{3,2,1,0:T(8,128)}, u32[]{:S(2)}, u32[]{:S(2)}) collective-permute-start(f32[1,3,256,256]{3,2,1,0:T(8,128)} %get-tuple-element.55), channel_id=1, source_target_pairs={{1,0},{2,1},{3,2},{4,3},{5,4},{6,5},{7,6},{8,7},{9,8},{10,9},{11,1... | collective-permute-start | bytes 2359304 | tf_op jit(solution)/shard_map/ppermute | solution.py:32
  191.8 5.8 %slice-start = ((f32[1,10,256,256]{3,2,1,0:T(8,128)}), f32[1,4,256,256]{3,2,1,0:T(8,128)S(1)}, s32[]{:S(2)}) async-start(f32[1,10,256,256]{3,2,1,0:T(8,128)} %reshape.291), calls=%async_computation.5 | async-start | bytes 2097152 | tf_op jit(solution)/shard_map/slice | solution.py:83
  276.6 117.1 %all-to-all-start.3 = ((f32[1,256,4,256]{3,2,0,1:T(4,128)}), f32[1,256,4,256]{3,2,0,1:T(4,128)}, u32[]{:S(2)}, u32[]{:S(2)}) async-start(f32[1,256,4,256]{3,2,0,1:T(4,128)} %copy.27), calls=%async_computation.3 | async-start | bytes 2097152 | tf_op jit(solution)/shard_map/all_to_all | solution.py:63
  286.2 212.0 %all-reduce.2.cloned.1.call-start = ((), (), s32[]{:S(2)}) async-start(), calls=%async_computation.4 | async-start | bytes 2097152 | tf_op jit(solution)/shard_map/psum | solution.py:105
  286.4 56.5 %collective-permute-start.4 = (f32[1,3,256,256]{3,2,1,0:T(8,128)S(1)}, f32[1,3,256,256]{3,2,1,0:T(8,128)S(1)}, u32[]{:S(2)}, u32[]{:S(2)}) collective-permute-start(f32[1,3,256,256]{3,2,1,0:T(8,128)S(1)} %get-tuple-element.57), channel_id=1, source_target_pairs={{0,1},{1,2},{2,3},{3,4},{4,5},{5,6},{6,7},{7,8},{8,9},{9,10},{10,1... | collective-permute-start | bytes 2359304 | tf_op jit(solution)/shard_map/ppermute | solution.py:20
  288.4 54.4 %collective-permute-start.5 = (f32[1,3,256,256]{3,2,1,0:T(8,128)S(1)}, f32[1,3,256,256]{3,2,1,0:T(8,128)S(1)}, u32[]{:S(2)}, u32[]{:S(2)}) collective-permute-start(f32[1,3,256,256]{3,2,1,0:T(8,128)S(1)} %get-tuple-element.58), channel_id=1, source_target_pairs={{1,0},{2,1},{3,2},{4,3},{5,4},{6,5},{7,6},{8,7},{9,8},{10,9},{11,1... | collective-permute-start | bytes 2359304 | tf_op jit(solution)/shard_map/ppermute | solution.py:22
  372.5 9.5 %copy-start.8 = (f32[3]{0:T(128)S(1)}, f32[3]{0:T(128)}, u32[]{:S(2)}) copy-start(f32[3]{0:T(128)} %param.19) | copy-start | bytes 40
  372.5 10.8 %copy-start.5 = (f32[1,4,256,256]{3,2,1,0:T(8,128)S(1)}, f32[1,4,256,256]{3,2,1,0:T(8,128)}, u32[]{:S(2)}) copy-start(f32[1,4,256,256]{3,2,1,0:T(8,128)} %get-tuple-element.65) | copy-start | bytes 3145732
  372.7 17.1 %collective-permute-start.6 = (f32[1,3,256,256]{3,2,1,0:T(8,128)S(1)}, f32[1,3,256,256]{3,2,1,0:T(8,128)S(1)}, u32[]{:S(2)}, u32[]{:S(2)}) collective-permute-start(f32[1,3,256,256]{3,2,1,0:T(8,128)S(1)} %get-tuple-element.54), channel_id=1, source_target_pairs={{63,0},{0,1},{1,2},{2,3},{3,4},{4,5},{5,6},{6,7},{7,8},{8,9},{9,10... | collective-permute-start | bytes 2359304 | tf_op jit(solution)/shard_map/ppermute | solution.py:32
  374.7 16.8 %collective-permute-start.7 = (f32[1,3,256,256]{3,2,1,0:T(8,128)S(1)}, f32[1,3,256,256]{3,2,1,0:T(8,128)S(1)}, u32[]{:S(2)}, u32[]{:S(2)}) collective-permute-start(f32[1,3,256,256]{3,2,1,0:T(8,128)S(1)} %get-tuple-element.53), channel_id=1, source_target_pairs={{1,0},{2,1},{3,2},{4,3},{5,4},{6,5},{7,6},{8,7},{9,8},{10,9},{11,1... | collective-permute-start | bytes 2359304 | tf_op jit(solution)/shard_map/ppermute | solution.py:32
  393.6 5.1 %copy-start.3 = (f32[1,4,256,256]{3,2,1,0:T(8,128)S(1)}, f32[1,4,256,256]{3,2,1,0:T(8,128)}, u32[]{:S(2)}) copy-start(f32[1,4,256,256]{3,2,1,0:T(8,128)} %param.14) | copy-start | bytes 3145732
  393.6 5.1 %copy-start.4 = (f32[4,256,256]{2,1,0:T(8,128)S(1)}, f32[4,256,256]{2,1,0:T(8,128)}, u32[]{:S(2)}) copy-start(f32[4,256,256]{2,1,0:T(8,128)} %param.15) | copy-start | bytes 3145732
  393.7 5.1 %copy-start.6 = (f32[1,4,256,256]{3,2,1,0:T(8,128)S(1)}, f32[1,4,256,256]{3,2,1,0:T(8,128)}, u32[]{:S(2)}) copy-start(f32[1,4,256,256]{3,2,1,0:T(8,128)} %get-tuple-element.65) | copy-start | bytes 3145732
Sparse Core Ops, SparseCore 0:
  405.5 92.7 all-reduce.1
where the time goes:
time: 508 us; the launch traced here: 507 us
  waiting for transfers between devices  194 us (38%)
  blocking collectives  134 us (26%)
  starting transfers between devices  56.7 us (11%)
  local copies, waits for them, and re-layouts  52.9 us (10%)
  other arithmetic  33.6 us (7%)
  matrix products  22.1 us (4%)
  between operations  14.4 us (3%)
    all_to_all x2, blocking collectives, apply_hamiltonian(): lax.all_to_all(vector, 'grid', split_axis=2, concat_axis=1, tiled=True)  134 us
    ppermute x2, waiting for transfers between devices, with_halo(): lax.ppermute(tail, axis, [(i, (i + 1) % count) for i in range(count)])  93.5 us
    psum x1, waiting for transfers between devices, local(): density = lax.psum(group_density, 'orb')  92.9 us
    scatter-add x2, other arithmetic, nonlocal_term(): jnp.zeros_like(flattened).at[:, ghost_index].add(spread)  24.9 us
    gather x2, local copies, waits for them, and re-layouts, nonlocal_term(): values = flattened[:, ghost_index].reshape(orb_count, per_dev, -1)  23.6 us
    all_to_all x2, starting transfers between devices, along_z(): lax.all_to_all(turned, 'grid', split_axis=1, concat_axis=2, tiled=True)  19.4 us
    ppermute x4, starting transfers between devices, from_behind(): return lax.ppermute(block, axis, route)  18.7 us
    ppermute x2, starting transfers between devices, with_halo(): lax.ppermute(head, axis, [((i + 1) % count, i) for i in range(count)])  14.5 us
  transfers between devices with their start and end apart: 11, of which 7 were waited for; matrix products, arithmetic and copies ran while one was open for 15% of the time, Pallas kernels for 0%

commit v1 on v0

--- a/solution.py
+++ b/solution.py
@@ -60,7 +60,12 @@
 
     def along_z(columns):
         turned = jnp.einsum("ozyx,zw->owyx", columns, kinetic_z, precision=PRECISE)
-        return lax.all_to_all(turned, "grid", split_axis=1, concat_axis=2, tiled=True)
+        return jnp.concatenate(
+            lax.all_to_all(
+                jnp.stack(jnp.split(turned, lax.axis_size("grid"), axis=1)), "grid", 0, 0
+            ),
+            axis=2,
+        )
 
     z_glob = sphere_cells[:, 0, :]
     in_plane = sphere_cells[:, 1, :]

time: 508 us -> 575 us (1.13)
  local copies, waits for them, and re-layouts: 52.9 us -> 119 us
    unnamed x23 -> x151, local copies, waits for them, and re-layouts: 4.65 us -> 80.9 us
    all_to_all x4 -> x0, local copies, waits for them, and re-layouts: 7.83 us -> none  [along_z(): lax.all_to_all(turned, 'grid', split_axis=1, concat_axis=2, tiled=True)]
  transfers between devices with their start and end apart: 11 -> 11, of which waited for: 7 -> 6; matrix products, arithmetic and copies ran while one was open for 15% -> 13% of each run, Pallas kernels for 0% -> 0%
where the time goes in v1:
time: 575 us; the launch traced here: 574 us
  waiting for transfers between devices  193 us (34%)
  blocking collectives  134 us (23%)
  local copies, waits for them, and re-layouts  119 us (21%)
  starting transfers between devices  56.8 us (10%)
  other arithmetic  34.7 us (6%)
  matrix products  22.1 us (4%)
  between operations  14.4 us (3%)
    all_to_all x2, blocking collectives, apply_hamiltonian(): lax.all_to_all(vector, 'grid', split_axis=2, concat_axis=1, tiled=True)  134 us
    ppermute x2, waiting for transfers between devices, with_halo(): lax.ppermute(tail, axis, [(i, (i + 1) % count) for i in range(count)])  93.5 us
    psum x1, waiting for transfers between devices, local(): density = lax.psum(group_density, 'orb')  92.4 us
    unnamed x151, local copies, waits for them, and re-layouts  80.9 us
    scatter-add x2, other arithmetic, nonlocal_term(): jnp.zeros_like(flattened).at[:, ghost_index].add(spread)  24.9 us
    gather x2, local copies, waits for them, and re-layouts, nonlocal_term(): values = flattened[:, ghost_index].reshape(orb_count, per_dev, -1)  23.6 us
    all_to_all x2, starting transfers between devices, along_z(): lax.all_to_all(jnp.stack(jnp.split(turned, lax.axis_size('grid'), axis=1)...  19.4 us
    ppermute x4, starting transfers between devices, from_behind(): return lax.ppermute(block, axis, route)  18.8 us
  transfers between devices with their start and end apart: 11, of which 6 were waited for; matrix products, arithmetic and copies ran while one was open for 13% of the time, Pallas kernels for 0%

profile of v1, /device:TPU:4, one launch (start us, length us, event | category | flops | bytes accessed | tf_op | source)
XLA Modules:
  0.0 573.9 jit_solution(2281132660657755700)
XLA Ops:
  8.4 70.6 %all_to_all.40 = f32[1,4,256,256]{3,1,0,2:T(4,128)S(1)} all-to-all(f32[1,4,256,256]{3,1,0,2:T(4,128)S(1)} %copy.20), channel_id=1, replica_groups=mesh['orb'=8,'grid'=64] {'grid'}, dimensions={2} | all-to-all | bytes 2097152 | tf_op jit(solution)/shard_map/all_to_all | solution.py:99
  79.6 2.1 convolution_bitcast_fusion.3
  120.6 9.8 %all-to-all-start.1 = ((f32[64,1,4,4,256]{4,2,3,1,0:T(4,128)}), f32[64,1,4,4,256]{4,2,3,1,0:T(4,128)}, u32[]{:S(2)}, u32[]{:S(2)}) async-start(f32[64,1,4,4,256]{4,2,3,1,0:T(4,128)} %constant_dynamic-update-slice_fusion), calls=%async_computation.1 | async-start | bytes 2097152 | tf_op jit(solution)/shard_map/all_to_all | solution.py:64
  131.4 2.0 collective-permute-start
  133.5 7.1 %collective-permute-start.1 = (f32[1,3,256,256]{3,2,1,0:T(8,128)S(1)}, f32[1,3,256,256]{3,2,1,0:T(8,128)S(1)}, u32[]{:S(2)}, u32[]{:S(2)}) collective-permute-start(f32[1,3,256,256]{3,2,1,0:T(8,128)S(1)} %get-tuple-element.60), channel_id=1, source_target_pairs={{1,0},{2,1},{3,2},{4,3},{5,4},{6,5},{7,6},{8,7},{9,8},{10,9},{11,1... | collective-permute-start | bytes 2359304 | tf_op jit(solution)/shard_map/ppermute | solution.py:22
  140.7 46.4 %collective-permute-done = f32[1,3,256,256]{3,2,1,0:T(8,128)S(1)} collective-permute-done((f32[1,3,256,256]{3,2,1,0:T(8,128)}, f32[1,3,256,256]{3,2,1,0:T(8,128)S(1)}, u32[]{:S(2)}, u32[]{:S(2)}) %collective-permute-start) | collective-permute-done | bytes 786464 | tf_op jit(solution)/shard_map/ppermute | solution.py:20
  188.6 11.8 %gather_fusion = f32[2048]{0:T(1024)S(1)} fusion(f32[655360]{0:T(1024)S(1)} %bitcast.671, s32[2048]{0:T(1024)S(1)} %broadcast_clamp_fusion), kind=kCustom, calls=%fused_computation | custom fusion | bytes 24576 | tf_op jit(solution)/shard_map/gather | solution.py:78
  201.0 11.9 %scatter_custom_fusion = f32[655360]{0:T(1024)S(1)} fusion(s32[2048]{0:T(1024)S(1)} %bitcast.681, f32[2048]{0:T(1024)S(1)} %bitcast.690, f32[]{:T(128)} %constant.158.clone.1), kind=kCustom, calls=%fused_computation.14 | custom fusion | flops 2048 | bytes 2621444 | tf_op jit(solution)/shard_map/scatter-add | solution.py:83
  214.8 2.8 fusion.109
  217.6 1.9 collective-permute-start.2
  219.5 7.4 %collective-permute-start.3 = (f32[1,3,256,256]{3,2,1,0:T(8,128)}, f32[1,3,256,256]{3,2,1,0:T(8,128)}, u32[]{:S(2)}, u32[]{:S(2)}) collective-permute-start(f32[1,3,256,256]{3,2,1,0:T(8,128)} %get-tuple-element.55), channel_id=1, source_target_pairs={{1,0},{2,1},{3,2},{4,3},{5,4},{6,5},{7,6},{8,7},{9,8},{10,9},{11,1... | collective-permute-start | bytes 2359304 | tf_op jit(solution)/shard_map/ppermute | solution.py:32
  227.0 2.1 convolution_bitcast_fusion.5
  230.4 4.4 collective-permute-done.2
  237.9 5.3 broadcast_multiply_fusion.1
  243.9 63.0 %all_to_all.41 = f32[1,4,256,256]{3,1,0,2:T(4,128)S(1)} all-to-all(f32[1,4,256,256]{3,1,0,2:T(4,128)S(1)} %copy.24), channel_id=1, replica_groups=mesh['orb'=8,'grid'=64] {'grid'}, dimensions={2} | all-to-all | bytes 2097152 | tf_op jit(solution)/shard_map/all_to_all | solution.py:99
  307.5 2.1 convolution_bitcast_fusion
  348.2 9.6 %all-to-all-start.3 = ((f32[64,1,4,4,256]{4,2,3,1,0:T(4,128)}), f32[64,1,4,4,256]{4,2,3,1,0:T(4,128)}, u32[]{:S(2)}, u32[]{:S(2)}) async-start(f32[64,1,4,4,256]{4,2,3,1,0:T(4,128)} %constant_dynamic-update-slice_fusion.64), calls=%async_computation.3 | async-start | bytes 2097152 | tf_op jit(solution)/shard_map/all_to_all | solution.py:64
  358.0 2.1 collective-permute-start.4
  360.1 7.3 %collective-permute-start.5 = (f32[1,3,256,256]{3,2,1,0:T(8,128)S(1)}, f32[1,3,256,256]{3,2,1,0:T(8,128)S(1)}, u32[]{:S(2)}, u32[]{:S(2)}) collective-permute-start(f32[1,3,256,256]{3,2,1,0:T(8,128)S(1)} %get-tuple-element.58), channel_id=1, source_target_pairs={{1,0},{2,1},{3,2},{4,3},{5,4},{6,5},{7,6},{8,7},{9,8},{10,9},{11,1... | collective-permute-start | bytes 2359304 | tf_op jit(solution)/shard_map/ppermute | solution.py:22
  367.4 47.1 %collective-permute-done.4 = f32[1,3,256,256]{3,2,1,0:T(8,128)S(1)} collective-permute-done((f32[1,3,256,256]{3,2,1,0:T(8,128)S(1)}, f32[1,3,256,256]{3,2,1,0:T(8,128)S(1)}, u32[]{:S(2)}, u32[]{:S(2)}) %collective-permute-start.4) | collective-permute-done | bytes 786464 | tf_op jit(solution)/shard_map/ppermute | solution.py:20
  416.1 11.8 %gather_fusion.1 = f32[2048]{0:T(1024)S(1)} fusion(f32[655360]{0:T(1024)S(1)} %bitcast.670, s32[2048]{0:T(1024)S(1)} %broadcast_clamp_fusion), kind=kCustom, calls=%fused_computation.1 | custom fusion | bytes 24576 | tf_op jit(solution)/shard_map/gather | solution.py:78
  428.4 12.9 %scatter_custom_fusion.1 = f32[655360]{0:T(1024)} fusion(s32[2048]{0:T(1024)S(1)} %bitcast.682, f32[2048]{0:T(1024)S(1)} %bitcast.689, f32[]{:T(128)} %constant.158.clone.1), kind=kCustom, calls=%fused_computation.12 | custom fusion | flops 2048 | bytes 2621444 | tf_op jit(solution)/shard_map/scatter-add | solution.py:83
  441.3 2.7 reshape.312
  444.3 2.2 collective-permute-start.6
  446.5 7.3 %collective-permute-start.7 = (f32[1,3,256,256]{3,2,1,0:T(8,128)S(1)}, f32[1,3,256,256]{3,2,1,0:T(8,128)S(1)}, u32[]{:S(2)}, u32[]{:S(2)}) collective-permute-start(f32[1,3,256,256]{3,2,1,0:T(8,128)S(1)} %get-tuple-element.53), channel_id=1, source_target_pairs={{1,0},{2,1},{3,2},{4,3},{5,4},{6,5},{7,6},{8,7},{9,8},{10,9},{11,1... | collective-permute-start | bytes 2359304 | tf_op jit(solution)/shard_map/ppermute | solution.py:32
  454.9 3.1 convolution_bitcast_fusion.1
  459.1 2.4 collective-permute-done.6
  461.5 2.1 fusion.24
  463.6 2.1 fusion.23
  465.8 6.5 %fusion.21 = f32[4,256,256]{2,1,0:T(8,128)} fusion(f32[1,4,256,256]{3,2,1,0:T(8,128)S(1)} %copy-done.3, f32[1,4,256,256]{3,2,1,0:T(8,128)} %fusion.23, f32[4,256,256]{2,1,0:T(8,128)S(1)} %copy-done.5, f32[1,4,256,256]{3,2,1,0:T(8,128)S(1)} %copy-done.7, f32[]{:T(128)} %bitcast.92, f32[]{:T(128)} %bitcast.91, f32[]{:T(128)} %bitcast, ...), kind=kOutput, calls=%fused_computation.35 | convolution fusion | flops 811270144 | bytes 7340044 | tf_op jit(solution)/shard_map/dot_general | solution.py:94
  472.3 92.4 %all-reduce.2.cloned.1.call-done = f32[4,256,256]{2,1,0:T(8,128)} async-done(((f32[4,256,256]{2,1,0:T(8,128)}), f32[4,256,256]{2,1,0:T(8,128)}) %all-reduce.2.cloned.1.call-update) | async-done | bytes 1048592 | tf_op jit(solution)/shard_map/psum | solution.py:110
  564.8 2.3 broadcast_multiply_fusion
  (187 shorter events, 94.7 us)
Async XLA Ops:
  6.5 193.9 %copy-start = (f32[16,4,128]{2,1,0:T(4,128)S(1)}, f32[16,4,128]{2,1,0:T(4,128)}, u32[]{:S(2)}) copy-start(f32[16,4,128]{2,1,0:T(4,128)} %param.17) | copy-start | bytes 98308
  81.6 48.8 %copy-start.1 = (f32[1,4,256,256]{3,2,1,0:T(8,128)S(1)}, f32[1,4,256,256]{3,2,1,0:T(8,128)}, u32[]{:S(2)}) copy-start(f32[1,4,256,256]{3,2,1,0:T(8,128)} %param.14) | copy-start | bytes 3145732
  120.6 20.0 %copy-start.8 = (s32[16,2,128]{2,1,0:T(2,128)S(1)}, s32[16,2,128]{2,1,0:T(2,128)}, u32[]{:S(2)}) copy-start(s32[16,2,128]{2,1,0:T(2,128)} %param.16) | copy-start | bytes 49156
  120.6 117.3 %all-to-all-start.1 = ((f32[64,1,4,4,256]{4,2,3,1,0:T(4,128)}), f32[64,1,4,4,256]{4,2,3,1,0:T(4,128)}, u32[]{:S(2)}, u32[]{:S(2)}) async-start(f32[64,1,4,4,256]{4,2,3,1,0:T(4,128)} %constant_dynamic-update-slice_fusion), calls=%async_computation.1 | async-start | bytes 2097152 | tf_op jit(solution)/shard_map/all_to_all | solution.py:64
  131.4 55.6 %collective-permute-start = (f32[1,3,256,256]{3,2,1,0:T(8,128)}, f32[1,3,256,256]{3,2,1,0:T(8,128)S(1)}, u32[]{:S(2)}, u32[]{:S(2)}) collective-permute-start(f32[1,3,256,256]{3,2,1,0:T(8,128)} %get-tuple-element.59), channel_id=1, source_target_pairs={{0,1},{1,2},{2,3},{3,4},{4,5},{5,6},{6,7},{7,8},{8,9},{9,10},{10,1... | collective-permute-start | bytes 2359304 | tf_op jit(solution)/shard_map/ppermute | solution.py:20
  133.5 53.6 %collective-permute-start.1 = (f32[1,3,256,256]{3,2,1,0:T(8,128)S(1)}, f32[1,3,256,256]{3,2,1,0:T(8,128)S(1)}, u32[]{:S(2)}, u32[]{:S(2)}) collective-permute-start(f32[1,3,256,256]{3,2,1,0:T(8,128)S(1)} %get-tuple-element.60), channel_id=1, source_target_pairs={{1,0},{2,1},{3,2},{4,3},{5,4},{6,5},{7,6},{8,7},{9,8},{10,9},{11,1... | collective-permute-start | bytes 2359304 | tf_op jit(solution)/shard_map/ppermute | solution.py:22
  188.6 12.1 %copy-start.10 = (f32[4]{0:T(128)S(1)}, f32[4]{0:T(128)}, u32[]{:S(2)}) copy-start(f32[4]{0:T(128)} %param.18) | copy-start | bytes 52
  214.8 12.2 %copy-start.2 = (f32[1,4,256,256]{3,2,1,0:T(8,128)S(1)}, f32[1,4,256,256]{3,2,1,0:T(8,128)}, u32[]{:S(2)}) copy-start(f32[1,4,256,256]{3,2,1,0:T(8,128)} %param.14) | copy-start | bytes 3145732
  217.6 17.2 %collective-permute-start.2 = (f32[1,3,256,256]{3,2,1,0:T(8,128)}, f32[1,3,256,256]{3,2,1,0:T(8,128)}, u32[]{:S(2)}, u32[]{:S(2)}) collective-permute-start(f32[1,3,256,256]{3,2,1,0:T(8,128)} %get-tuple-element.56), channel_id=1, source_target_pairs={{63,0},{0,1},{1,2},{2,3},{3,4},{4,5},{5,6},{6,7},{7,8},{8,9},{9,10... | collective-permute-start | bytes 2359304 | tf_op jit(solution)/shard_map/ppermute | solution.py:32
  219.5 17.1 %collective-permute-start.3 = (f32[1,3,256,256]{3,2,1,0:T(8,128)}, f32[1,3,256,256]{3,2,1,0:T(8,128)}, u32[]{:S(2)}, u32[]{:S(2)}) collective-permute-start(f32[1,3,256,256]{3,2,1,0:T(8,128)} %get-tuple-element.55), channel_id=1, source_target_pairs={{1,0},{2,1},{3,2},{4,3},{5,4},{6,5},{7,6},{8,7},{9,8},{10,9},{11,1... | collective-permute-start | bytes 2359304 | tf_op jit(solution)/shard_map/ppermute | solution.py:32
  229.1 5.8 %slice-start = ((f32[1,10,256,256]{3,2,1,0:T(8,128)}), f32[1,4,256,256]{3,2,1,0:T(8,128)S(1)}, s32[]{:S(2)}) async-start(f32[1,10,256,256]{3,2,1,0:T(8,128)} %reshape.305), calls=%async_computation.5 | async-start | bytes 2097152 | tf_op jit(solution)/shard_map/slice | solution.py:88
  348.2 117.6 %all-to-all-start.3 = ((f32[64,1,4,4,256]{4,2,3,1,0:T(4,128)}), f32[64,1,4,4,256]{4,2,3,1,0:T(4,128)}, u32[]{:S(2)}, u32[]{:S(2)}) async-start(f32[64,1,4,4,256]{4,2,3,1,0:T(4,128)} %constant_dynamic-update-slice_fusion.64), calls=%async_computation.3 | async-start | bytes 2097152 | tf_op jit(solution)/shard_map/all_to_all | solution.py:64
  357.8 207.0 %all-reduce.2.cloned.1.call-start = ((), (), s32[]{:S(2)}) async-start(), calls=%async_computation.4 | async-start | bytes 2097152 | tf_op jit(solution)/shard_map/psum | solution.py:110
  358.0 56.5 %collective-permute-start.4 = (f32[1,3,256,256]{3,2,1,0:T(8,128)S(1)}, f32[1,3,256,256]{3,2,1,0:T(8,128)S(1)}, u32[]{:S(2)}, u32[]{:S(2)}) collective-permute-start(f32[1,3,256,256]{3,2,1,0:T(8,128)S(1)} %get-tuple-element.57), channel_id=1, source_target_pairs={{0,1},{1,2},{2,3},{3,4},{4,5},{5,6},{6,7},{7,8},{8,9},{9,10},{10,1... | collective-permute-start | bytes 2359304 | tf_op jit(solution)/shard_map/ppermute | solution.py:20
  360.1 54.4 %collective-permute-start.5 = (f32[1,3,256,256]{3,2,1,0:T(8,128)S(1)}, f32[1,3,256,256]{3,2,1,0:T(8,128)S(1)}, u32[]{:S(2)}, u32[]{:S(2)}) collective-permute-start(f32[1,3,256,256]{3,2,1,0:T(8,128)S(1)} %get-tuple-element.58), channel_id=1, source_target_pairs={{1,0},{2,1},{3,2},{4,3},{5,4},{6,5},{7,6},{8,7},{9,8},{10,9},{11,1... | collective-permute-start | bytes 2359304 | tf_op jit(solution)/shard_map/ppermute | solution.py:22
  444.1 13.9 %copy-start.4 = (f32[1,10,256,256]{3,2,1,0:T(8,128)}, f32[1,10,256,256]{3,2,1,0:T(8,128)S(1)}, u32[]{:S(2)}) copy-start(f32[1,10,256,256]{3,2,1,0:T(8,128)S(1)} %reshape.312) | copy-start | bytes 7864324
  444.1 9.7 %copy-start.9 = (f32[3]{0:T(128)S(1)}, f32[3]{0:T(128)}, u32[]{:S(2)}) copy-start(f32[3]{0:T(128)} %param.19) | copy-start | bytes 40
  444.1 10.8 %copy-start.6 = (f32[1,4,256,256]{3,2,1,0:T(8,128)S(1)}, f32[1,4,256,256]{3,2,1,0:T(8,128)}, u32[]{:S(2)}) copy-start(f32[1,4,256,256]{3,2,1,0:T(8,128)} %get-tuple-element.65) | copy-start | bytes 3145732
  444.3 17.2 %collective-permute-start.6 = (f32[1,3,256,256]{3,2,1,0:T(8,128)S(1)}, f32[1,3,256,256]{3,2,1,0:T(8,128)S(1)}, u32[]{:S(2)}, u32[]{:S(2)}) collective-permute-start(f32[1,3,256,256]{3,2,1,0:T(8,128)S(1)} %get-tuple-element.54), channel_id=1, source_target_pairs={{63,0},{0,1},{1,2},{2,3},{3,4},{4,5},{5,6},{6,7},{7,8},{8,9},{9,10... | collective-permute-start | bytes 2359304 | tf_op jit(solution)/shard_map/ppermute | solution.py:32
  446.5 17.1 %collective-permute-start.7 = (f32[1,3,256,256]{3,2,1,0:T(8,128)S(1)}, f32[1,3,256,256]{3,2,1,0:T(8,128)S(1)}, u32[]{:S(2)}, u32[]{:S(2)}) collective-permute-start(f32[1,3,256,256]{3,2,1,0:T(8,128)S(1)} %get-tuple-element.53), channel_id=1, source_target_pairs={{1,0},{2,1},{3,2},{4,3},{5,4},{6,5},{7,6},{8,7},{9,8},{10,9},{11,1... | collective-permute-start | bytes 2359304 | tf_op jit(solution)/shard_map/ppermute | solution.py:32
  459.0 6.7 %copy-start.3 = (f32[1,4,256,256]{3,2,1,0:T(8,128)S(1)}, f32[1,4,256,256]{3,2,1,0:T(8,128)}, u32[]{:S(2)}) copy-start(f32[1,4,256,256]{3,2,1,0:T(8,128)} %param.14) | copy-start | bytes 3145732
  459.1 6.7 %copy-start.5 = (f32[4,256,256]{2,1,0:T(8,128)S(1)}, f32[4,256,256]{2,1,0:T(8,128)}, u32[]{:S(2)}) copy-start(f32[4,256,256]{2,1,0:T(8,128)} %param.15) | copy-start | bytes 3145732
  459.1 6.7 %copy-start.7 = (f32[1,4,256,256]{3,2,1,0:T(8,128)S(1)}, f32[1,4,256,256]{3,2,1,0:T(8,128)}, u32[]{:S(2)}) copy-start(f32[1,4,256,256]{3,2,1,0:T(8,128)} %get-tuple-element.65) | copy-start | bytes 3145732
Sparse Core Ops, SparseCore 0:
  472.5 92.2 all-reduce.1
